TPU v7x, 1024 devices: a whole 4x4x32 slice. The times are simulated.
1024 devices in a mesh: rows: 64 (over y_hi, z), cols: 16 (over x, y_lo, core).
Axes of the slice: x: 4, y: 4 (y_hi: 2, y_lo: 2; y = y_hi * 2 + y_lo), z: 32, core: 2. Of those that a mesh axis runs over, the one named last changes fastest.
Arguments:
- features: float32 [131072, 256], P(('rows', 'cols')), may hold values from -6 to 6
- degrees: int32 [131072], P(('rows', 'cols')), may hold values from 1 to 16
- tiles: float32 [1024, 24, 128, 128], P(('rows', 'cols')), may hold values from -0.125 to 0.125
- coords: int32 [1024, 24], P(('rows', 'cols')), may hold values from 0 to 16
- counts: int32 [1024], P(('rows', 'cols')), may hold values from 1 to 24, as said below
- weight: float32 [256, 256], replicated, may hold values from -0.375 to 0.375
- cotangent: float32 [131072, 256], P(('rows', 'cols')), may hold values from -6 to 6
Outputs:
- hidden: float32 [131072, 256], P(('rows', 'cols'))
- feature_grad: float32 [131072, 256], P(('rows', 'cols'))
- weight_grad: float32 [256, 256], replicated
Inputs may be any that keep to these rules, and one draw needn't show every extreme that they name: `coords`: entries past a slab's count are unused. `counts`: some slab has all 24 tiles live.
All inputs are finite; a program needn't handle non-finite values.
Results may differ from a plain program's by a relative error of at most 0.0003.
Values sent between devices are 32-bit elements; how exact they have to be, the bound alone decides.
A program may use at most 32 MiB of HBM per device.

v0:
```python
import jax
import jax.numpy as jnp
from jax import lax
from jax.sharding import PartitionSpec as P


def shifted(value, axis, steps):
    count = lax.axis_size(axis)
    pairs = [(source, (source + steps) % count) for source in range(count)]
    return lax.ppermute(value, axis, pairs)


def roll_rows(values, offset):
    return shifted(values, "rows", offset)


def local(features, degrees, tiles, coords, counts, weight, cotangent):
    high = lax.Precision.HIGHEST
    tile_size = tiles.shape[2]
    slots = tiles.shape[1]
    ncols = lax.axis_size("cols")
    norm = (1.0 / jnp.sqrt(degrees.astype(jnp.float32)))[:, None]
    scaled = features * norm
    tile_block = tiles[0]
    where_col = coords[0]
    live_tiles = jnp.arange(slots, dtype=jnp.int32) < counts[0]
    nearby = ((where_col == ncols) & live_tiles).astype(jnp.float32)
    select = (
        (where_col[None, :] == jnp.arange(ncols, dtype=jnp.int32)[:, None]) & live_tiles[None, :]
    ).astype(jnp.float32)
    col_blocks = jnp.einsum("jk,kit->jit", select, tile_block, precision=high)
    row_matrix = jnp.transpose(col_blocks, (1, 0, 2)).reshape(tile_size, ncols * tile_size)
    near_matrix = jnp.einsum("k,kit->it", nearby, tile_block, precision=high)
    following = roll_rows(scaled, -1)
    columns = row_matrix
    gathered = jnp.dot(columns, lax.all_gather(scaled, "cols", axis=0, tiled=True), precision=high)
    gathered = gathered + jnp.dot(near_matrix, following, precision=high)
    aggregated = gathered * norm
    pre = jnp.dot(aggregated, weight, precision=high)
    gate = jax.nn.sigmoid(pre)
    hidden = pre * gate
    pre_grad = cotangent * gate * (1.0 + pre * (1.0 - gate))
    weight_grad = lax.psum(jnp.dot(aggregated.T, pre_grad, precision=high), ("rows", "cols"))
    agg_grad = jnp.dot(pre_grad, weight.T, precision=high) * norm
    columns = row_matrix
    mine = lax.psum_scatter(
        jnp.dot(columns.T, agg_grad, precision=high), "cols", scatter_dimension=0, tiled=True
    )
    near_term = jnp.dot(near_matrix.T, agg_grad, precision=high)
    feature_grad = (mine + roll_rows(near_term, 1)) * norm
    return (hidden, feature_grad, weight_grad)


def solution(mesh):
    return jax.shard_map(
        local,
        mesh=mesh,
        in_specs=(
            P(("rows", "cols"), None),
            P(("rows", "cols")),
            P(("rows", "cols"), None, None, None),
            P(("rows", "cols"), None),
            P(("rows", "cols")),
            P(),
            P(("rows", "cols"), None),
        ),
        out_specs=(P(("rows", "cols"), None), P(("rows", "cols"), None), P()),
        check_vma=False,
    )
```

profile of v0, /device:TPU:1, one launch (start us, length us, event | category | flops | bytes accessed | tf_op | source)
XLA Modules:
  0.0 1042.2 jit_solution(3815597586344294709)
XLA Ops:
  7.2 0.0 copy-start
  7.2 0.0 copy-start.2
  7.2 0.0 all-gather.2.cloned.1.call-start
  7.2 0.8 convert_rsqrt_fusion
  8.0 1.6 broadcast_multiply_fusion
  9.7 0.0 all-gather.2.cloned.1.call-update
  9.7 0.0 reduce-scatter.2.cloned.1.call-start
  9.7 21.9 %collective-permute-start = (f32[128,256]{1,0:T(8,128)}, f32[128,256]{1,0:T(8,128)S(1)}, u32[]{:S(2)}, u32[]{:S(2)}) collective-permute-start(f32[128,256]{1,0:T(8,128)} %broadcast_multiply_fusion), channel_id=1, source_target_pairs={{0,1008},{16,0},{32,16},{48,32},{64,48},{80,64},{96,80},{112,96},{... | collective-permute-start | bytes 393224 | tf_op jit(solution)/shard_map/ppermute | solution.py:10
  32.3 0.0 copy-done
  32.3 2.1 fusion
  34.4 0.0 copy-done.2
  34.4 1.6 fusion.2
  36.0 35.9 %all-gather.2.cloned.1.call-done = f32[2048,256]{1,0:T(8,128)} async-done(((f32[128,256]{1,0:T(8,128)}), f32[2048,256]{1,0:T(8,128)}) %all-gather.2.cloned.1.call-update) | async-done | bytes 2097168 | tf_op jit(solution)/shard_map/all_gather | solution.py:36
  71.9 2.9 fusion.7
  74.8 0.0 collective-permute-done
  74.9 0.3 fusion.4
  75.1 0.0 copy-done.1
  75.1 1.0 fusion.11
  76.1 0.0 copy-done.3
  76.1 0.4 convolution_multiply_fusion
  76.5 3.2 fusion.5
  79.7 0.0 reduce-scatter.2.cloned.1.call-update
  79.7 0.0 all-reduce.2.cloned.1.call-start
  79.8 0.3 fusion.26
  80.1 3.3 collective-permute-start.1
  83.4 1.1 fusion.25
  84.5 0.0 all-reduce.2.cloned.1.call-update
  84.5 8.6 collective-permute-done.1
  93.1 67.2 %reduce-scatter.2.cloned.1.call-done = f32[128,256]{1,0:T(8,128)} async-done(((f32[2048,256]{1,0:T(8,128)}), f32[128,256]{1,0:T(8,128)}) %reduce-scatter.2.cloned.1.call-update) | async-done | bytes 131088 | tf_op jit(solution)/shard_map/reduce_scatter | solution.py:46
  160.3 1.6 add_multiply_fusion
  162.0 872.1 %all-reduce.2.cloned.1.call-done = f32[256,256]{1,0:T(8,128)} async-done(((f32[256,256]{1,0:T(8,128)}), f32[256,256]{1,0:T(8,128)}) %all-reduce.2.cloned.1.call-update) | async-done | bytes 262160 | tf_op jit(solution)/shard_map/psum | solution.py:43
  1034.0 1.7 copy.27
  (3 shorter events, 0.0 us)
Async XLA Ops:
  7.2 25.1 %copy-start = (f32[1,24,128,128]{3,2,1,0:T(8,128)S(1)}, f32[1,24,128,128]{3,2,1,0:T(8,128)}, u32[]{:S(2)}) copy-start(f32[1,24,128,128]{3,2,1,0:T(8,128)} %param.9) | copy-start | bytes 4718596
  7.2 27.2 %copy-start.2 = (s32[1,24]{1,0:T(1,128)S(1)}, s32[1,24]{1,0:T(1,128)}, u32[]{:S(2)}) copy-start(s32[1,24]{1,0:T(1,128)} %param.10) | copy-start | bytes 292
  7.2 64.7 %all-gather.2.cloned.1.call-start = ((), (), s32[]{:S(2)}) async-start(), calls=%async_computation.1 | async-start | bytes 2228224 | tf_op jit(solution)/shard_map/all_gather | solution.py:36
  9.7 150.6 %reduce-scatter.2.cloned.1.call-start = ((), (), s32[]{:S(2)}) async-start(), calls=%async_computation.2 | async-start | bytes 2228224 | tf_op jit(solution)/shard_map/reduce_scatter | solution.py:46
  9.7 65.1 %collective-permute-start = (f32[128,256]{1,0:T(8,128)}, f32[128,256]{1,0:T(8,128)S(1)}, u32[]{:S(2)}, u32[]{:S(2)}) collective-permute-start(f32[128,256]{1,0:T(8,128)} %broadcast_multiply_fusion), channel_id=1, source_target_pairs={{0,1008},{16,0},{32,16},{48,32},{64,48},{80,64},{96,80},{112,96},{... | collective-permute-start | bytes 393224 | tf_op jit(solution)/shard_map/ppermute | solution.py:10
  71.9 3.2 copy-start.1
  71.9 4.2 copy-start.3
  79.7 954.3 %all-reduce.2.cloned.1.call-start = ((), (), s32[]{:S(2)}) async-start(), calls=%async_computation.3 | async-start | bytes 524288 | tf_op jit(solution)/shard_map/psum | solution.py:43
  80.1 13.0 %collective-permute-start.1 = (f32[128,256]{1,0:T(8,128)S(1)}, f32[128,256]{1,0:T(8,128)S(1)}, u32[]{:S(2)}, u32[]{:S(2)}) collective-permute-start(f32[128,256]{1,0:T(8,128)S(1)} %fusion.26), channel_id=1, source_target_pairs={{0,16},{16,32},{32,48},{48,64},{64,80},{80,96},{96,112},{112,128},... | collective-permute-start | bytes 393224 | tf_op jit(solution)/shard_map/ppermute | solution.py:10
Sparse Core Ops, SparseCore 0:
  11.3 60.5 all-gather.1
  79.8 80.4 reduce-scatter.1
  166.3 867.6 all-reduce.1
where the time goes:
time: 1040 us
  waiting for transfers between devices  984 us (95%)
  starting transfers between devices  25.2 us (2%)
  between operations  14.5 us (1%)
  matrix products  12.9 us (1%)
    psum x1, waiting for transfers between devices, local(): lax.psum(jnp.dot(aggregated.T, pre_grad, precision=high), ('rows', 'cols'))  872 us
    reduce_scatter x1, waiting for transfers between devices, local(): lax.psum_scatter(jnp.dot(columns.T, agg_grad, precision=high), 'cols', sc...  67.2 us
    all_gather x1, waiting for transfers between devices, local(): lax.all_gather(scaled, 'cols', axis=0, tiled=True)  35.9 us
    ppermute x2, starting transfers between devices, shifted(): return lax.ppermute(value, axis, pairs)  25.1 us
  transfers between devices with their start and end apart: 5, of which 4 were waited for; matrix products, arithmetic and copies ran while one was open for 1% of the time, Pallas kernels for 0%

commit v1 on v0

v1 whole, which is shorter than its diff:
```python
import jax
import jax.numpy as jnp
from jax import lax
from jax.experimental import pallas as pl
from jax.experimental.pallas import tpu as pltpu
from jax.sharding import PartitionSpec as P

F = 256
T = 128
SLOTS = 24
ROWS = 64
NCOLS = 16
HIGH = lax.Precision.HIGHEST
MESH = pl.DeviceIdType.MESH
f32 = jnp.float32

PLANE = [(h, x, y) for h in range(2) for x in range(4) for y in range(2) if (h, x, y) != (0, 0, 0)]
CHIPS = [(x, y) for x in range(4) for y in range(2) if (x, y) != (0, 0)]


def dot(a, b, ca=1, cb=0):
    return lax.dot_general(a, b, (((ca,), (cb,)), ((), ())), precision=HIGH, preferred_element_type=f32)


def kernel(
    deg, coords, counts, feat, tiles, weight, cot,
    hid_o, fg_o, wg_o,
    X, XN, TV, A, FV, WV, CV, NB, AGG, PG, G, HID,
    WP, WR, WS, R1, ZA, ZB, FW,
    TS, TO, RB, RC, TN, RN, FGV,
    lsem, xsend, xrecv, nsend, nrecv, wsend, wrecv, psend, precv,
    zasend, zarecv, zbsend, zbrecv, fsend, frecv, tsend, trecv, csend, crecv, osem, chain,
):
    r = lax.axis_index("rows")
    c = lax.axis_index("cols")
    h, z = r // 32, r % 32
    x, y, k = c // 4, (c // 2) % 2, c % 2

    def dev(dh=0, dx=0, dy=0, dc=0, dz=0):
        row = ((h + dh) % 2) * 32 + (z + dz) % 32
        col = ((x + dx) % 4) * 4 + ((y + dy) % 2) * 2 + (k + dc) % 2
        return row, col

    def slot(dx=0, dy=0, dc=0):
        return ((x + dx) % 4) * 4 + ((y + dy) % 2) * 2 + (k + dc) % 2

    def remote(src, dst, ss, rs, to):
        return pltpu.make_async_remote_copy(
            src_ref=src, dst_ref=dst, send_sem=ss, recv_sem=rs, device_id=to, device_id_type=MESH
        )

    pending = []

    def start(src, dst, ss, rs, to):
        cp = remote(src, dst, ss, rs, to)
        cp.start()
        pending.append(cp)

    SIB = dev(dc=1)
    nxt = ((r + 1) % ROWS, c)
    prv = ((r + ROWS - 1) % ROWS, c)

    loads = [
        pltpu.make_async_copy(feat, FV, lsem.at[0]),
        pltpu.make_async_copy(tiles, TV, lsem.at[1]),
        pltpu.make_async_copy(weight, WV, lsem.at[2]),
        pltpu.make_async_copy(cot, CV, lsem.at[3]),
    ]
    for cp in loads:
        cp.start()

    barrier = pltpu.get_barrier_semaphore()
    greet = [dev(dh=a, dx=b, dy=d) for a, b, d in PLANE]
    greet += [SIB, nxt, prv, dev(dz=1), dev(dz=31)]
    for to in greet:
        pl.semaphore_signal(barrier, inc=1, device_id=to, device_id_type=MESH)

    nrow = 1.0 / jnp.sqrt(deg[...].astype(f32))
    eye = lax.broadcasted_iota(jnp.int32, (T, T), 0) == lax.broadcasted_iota(jnp.int32, (T, T), 1)
    norm = jnp.sum(jnp.where(eye, jnp.broadcast_to(nrow, (T, T)), 0.0), axis=1, keepdims=True)
    NB[...] = jnp.broadcast_to(norm, (T, F))
    me = slot()
    loads[0].wait()
    X[me] = FV[...] * NB[...]
    pl.semaphore_wait(barrier, len(greet))

    half = T // 2

    def piece(sl, hf):
        return X.at[sl, pl.ds(hf * half, half)]

    def send(sl, hf, to):
        start(piece(sl, hf), piece(sl, hf), xsend.at[len(pending)], xrecv.at[sl, hf], to)

    def recv(sl, hf):
        remote(piece(sl, hf), piece(sl, hf), xsend.at[0], xrecv.at[sl, hf], SIB).wait_recv()

    def step(level):
        if level > 0:
            pl.semaphore_wait(chain.at[level - 1], 2)
        if level < 4:
            d = 2 ** level
            for dz in (d, 32 - d):
                pl.semaphore_signal(chain.at[level], inc=1, device_id=dev(dz=dz), device_id_type=MESH)

    def use(sl):
        AGG[...] += dot(A[sl], X[sl])

    R, L, Y = dev(dx=1), dev(dx=3), dev(dy=1)
    send(me, 0, Y)
    send(me, 1, Y)
    send(me, 0, R)
    send(me, 1, L)
    send(me, 1, R)
    send(me, 0, L)
    for hf in (0, 1):
        send(me, hf, SIB)
    start(X.at[me], XN, nsend.at[0], nrecv.at[0], prv)
    step(0)

    loads[1].wait()
    live = counts[0]

    def build(j, carry):
        acc = jnp.zeros((T, T), f32)
        for t in range(SLOTS):
            on = jnp.logical_and(coords[0, t] == j, t < live)
            acc = acc + jnp.where(on, 1.0, 0.0) * TV[t]
        A[j] = acc
        return carry

    lax.fori_loop(0, NCOLS + 1, build, 0)
    AGG[...] = dot(A[me], X[me])

    ys = slot(dy=1)
    recv(ys, 0)
    send(ys, 0, R)
    recv(ys, 1)
    send(ys, 1, L)
    send(ys, 1, R)
    send(ys, 0, L)
    for hf in (0, 1):
        send(ys, hf, SIB)
    step(1)
    done = [ys]
    for dy in (0, 1):
        a, b = slot(dx=3, dy=dy), slot(dx=1, dy=dy)
        recv(a, 0)
        send(a, 0, R)
        recv(b, 1)
        send(b, 1, L)
        send(a, 0, SIB)
        send(b, 1, SIB)
        recv(a, 1)
        send(a, 1, SIB)
        recv(b, 0)
        send(b, 0, SIB)
        step(2 + dy)
        for sl in done:
            use(sl)
        done = [a, b]
    for dy in (0, 1):
        sl = slot(dx=2, dy=dy)
        for hf in (0, 1):
            recv(sl, hf)
            send(sl, hf, SIB)
        done.append(sl)
    for sl in done:
        use(sl)
    remote(X.at[me], XN, nsend.at[0], nrecv.at[0], prv).wait_recv()
    AGG[...] += dot(A[NCOLS], XN[...])
    for dx, dy in [(0, 0), (0, 1), (3, 0), (1, 0), (3, 1), (1, 1), (2, 0), (2, 1)]:
        sl = slot(dx=dx, dy=dy, dc=1)
        for hf in (0, 1):
            recv(sl, hf)
        use(sl)

    loads[2].wait()
    loads[3].wait()
    agg = AGG[...] * NB[...]
    pre = dot(agg, WV[...])
    gate = jax.nn.sigmoid(pre)
    HID[...] = pre * gate
    hid_copy = pltpu.make_async_copy(HID, hid_o, osem.at[0])
    hid_copy.start()
    pg = CV[...] * gate * (1.0 + pre * (1.0 - gate))
    PG[...] = pg
    wg = dot(agg, pg, 0, 0)
    WP[0] = wg[:T]
    WP[1] = wg[T:]
    start(WP.at[1 - k], WR, wsend.at[0], wrecv.at[0], SIB)
    G[...] = dot(PG[...], WV[...], 1, 1) * NB[...]
    TN[...] = dot(A[NCOLS], G[...], 0, 0)
    start(TN, RN, nsend.at[1], nrecv.at[1], nxt)
    remote(WP.at[0], WR, wsend.at[0], wrecv.at[0], SIB).wait_recv()
    WS[...] = (WP[k] + WR[...]).reshape(16, 8, F)

    def plane_id(dh=0, dx=0, dy=0):
        return ((x + dx) % 4) * 4 + ((h + dh) % 2) * 2 + (y + dy) % 2

    q = plane_id()
    for i, (a, b, d) in enumerate(PLANE):
        start(WS.at[plane_id(a, b, d)], R1.at[i], psend.at[i], precv.at[i], dev(dh=a, dx=b, dy=d))

    for p in range(8):
        TS[p] = dot(A[p * 2 + 1 - k], G[...], 0, 0)
        start(TS.at[p], RB.at[p], tsend.at[p], trecv.at[p], SIB)
    for p in range(8):
        TO[p] = dot(A[p * 2 + k], G[...], 0, 0)

    for i in range(15):
        remote(WS.at[0], R1.at[i], psend.at[i], precv.at[i], SIB).wait_recv()
    total = WS[q]
    for i in range(15):
        total = total + R1[i]
    z4, zs = z % 4, z // 4
    ZA[z4] = total
    for i in range(1, 4):
        m = (z4 + i) % 4
        start(ZA.at[z4], ZA.at[z4], zasend.at[i - 1], zarecv.at[z4], (h * 32 + zs * 4 + m, c))
    step(4)
    for p in range(8):
        remote(TS.at[p], RB.at[p], tsend.at[p], trecv.at[p], SIB).wait_recv()
        TO[p] = TO[p] + RB[p]
    for i in range(1, 4):
        m = (z4 + i) % 4
        remote(ZA.at[m], ZA.at[m], zasend.at[0], zarecv.at[m], SIB).wait_recv()
    ZB[zs] = ((ZA[0] + ZA[1]) + (ZA[2] + ZA[3]))
    for i in range(1, 8):
        start(ZB.at[zs], ZB.at[zs], zbsend.at[i - 1], zbrecv.at[zs], dev(dz=4 * i))

    cp_id = x * 2 + y
    for i, (dx, dy) in enumerate(CHIPS):
        to = ((x + dx) % 4) * 2 + (y + dy) % 2
        start(TO.at[to], RC.at[i], csend.at[i], crecv.at[i], dev(dx=dx, dy=dy))

    for i in range(1, 8):
        m = (zs + i) % 8
        remote(ZB.at[m], ZB.at[m], zbsend.at[0], zbrecv.at[m], SIB).wait_recv()
    total = ZB[0]
    for i in range(1, 8):
        total = total + ZB[i]
    FW[k * 16 + q] = total
    mine = FW.at[k * 16 + q]
    for i, (a, b, d) in enumerate(PLANE):
        start(mine, mine, fsend.at[i], frecv.at[q], dev(dh=a, dx=b, dy=d))

    remote(TN, RN, nsend.at[1], nrecv.at[1], nxt).wait_recv()
    for i in range(7):
        remote(TO.at[0], RC.at[i], csend.at[i], crecv.at[i], SIB).wait_recv()
    fg = TO[cp_id] + RN[...]
    for i in range(7):
        fg = fg + RC[i]
    FGV[...] = fg * NB[...]
    fg_copy = pltpu.make_async_copy(FGV, fg_o, osem.at[1])
    fg_copy.start()

    for a, b, d in PLANE:
        o = plane_id(a, b, d)
        part = FW.at[k * 16 + o]
        remote(part, part, fsend.at[0], frecv.at[o], SIB).wait_recv()
    block = FW.at[pl.ds(k * 16, 16)]
    start(block, block, wsend.at[1], wrecv.at[1], SIB)
    other = FW.at[pl.ds((1 - k) * 16, 16)]
    remote(other, other, wsend.at[1], wrecv.at[1], SIB).wait_recv()
    wg_copy = pltpu.make_async_copy(FW, wg_o, osem.at[2])
    wg_copy.start()
    hid_copy.wait()
    fg_copy.wait()
    for cp in pending:
        cp.wait_send()
    wg_copy.wait()


def local(features, degrees, tiles, coords, counts, weight, cotangent):
    anyspace = pl.BlockSpec(memory_space=pl.ANY)
    smem = pl.BlockSpec(memory_space=pltpu.SMEM)
    vmem = pl.BlockSpec(memory_space=pltpu.VMEM)
    D = pltpu.SemaphoreType.DMA
    V = lambda *s: pltpu.VMEM(s, f32)
    hidden, feature_grad, weight_grad = pl.pallas_call(
        kernel,
        out_shape=(
            jax.ShapeDtypeStruct((T, F), f32),
            jax.ShapeDtypeStruct((T, F), f32),
            jax.ShapeDtypeStruct((32, 8, F), f32),
        ),
        in_specs=[vmem, smem, smem, anyspace, anyspace, anyspace, anyspace],
        out_specs=(anyspace, anyspace, anyspace),
        scratch_shapes=[
            V(NCOLS, T, F), V(T, F), V(SLOTS, T, T), V(NCOLS + 1, T, T), V(T, F), V(F, F), V(T, F),
            V(T, F), V(T, F), V(T, F), V(T, F), V(T, F),
            V(2, T, F), V(T, F), V(16, 8, F), V(15, 8, F), V(4, 8, F), V(8, 8, F), V(32, 8, F),
            V(8, T, F), V(8, T, F), V(8, T, F), V(7, T, F), V(T, F), V(T, F), V(T, F),
            D((4,)), D((48,)), D((NCOLS, 2)), D((2,)), D((2,)), D((2,)), D((2,)), D((15,)), D((15,)),
            D((3,)), D((4,)), D((7,)), D((8,)), D((15,)), D((16,)), D((8,)), D((8,)), D((7,)), D((7,)),
            D((3,)), pltpu.SemaphoreType.REGULAR((4,)),
        ],
        compiler_params=pltpu.CompilerParams(
            collective_id=1, has_side_effects=True, vmem_limit_bytes=60 << 20
        ),
        cost_estimate=pl.CostEstimate(flops=400_000_000, bytes_accessed=3_000_000, transcendentals=32768),
        name="layer",
    )(degrees.reshape(1, T), coords, counts, features, tiles.reshape(SLOTS, T, T), weight, cotangent)
    return hidden, feature_grad, weight_grad.reshape(F, F)


def solution(mesh):
    return jax.shard_map(
        local,
        mesh=mesh,
        in_specs=(
            P(("rows", "cols"), None),
            P(("rows", "cols")),
            P(("rows", "cols"), None, None, None),
            P(("rows", "cols"), None),
            P(("rows", "cols")),
            P(),
            P(("rows", "cols"), None),
        ),
        out_specs=(P(("rows", "cols"), None), P(("rows", "cols"), None), P()),
        check_vma=False,
    )
```

time: 1040 us -> 79.7 us (0.08)
  waiting for transfers between devices: 984 us -> 0 us
  Pallas kernels: 0 us -> 73.4 us
  starting transfers between devices: 25.2 us -> 0 us
  between operations: 14.5 us -> 1.29 us
  matrix products: 12.9 us -> 0 us
    psum x1 -> x0, waiting for transfers between devices: 872 us -> none  [local(): lax.psum(jnp.dot(aggregated.T, pre_grad, precision=high), ('rows', 'cols'))]
    pallas_call x0 -> x1, Pallas kernels: none -> 73.4 us  [local(): pl.pallas_call(kernel, out_shape=(jax.ShapeDtypeStruct((T, F), f32), jax....]
    reduce_scatter x1 -> x0, waiting for transfers between devices: 67.2 us -> none  [local(): lax.psum_scatter(jnp.dot(columns.T, agg_grad, precision=high), 'cols', sc...]
    all_gather x1 -> x0, waiting for transfers between devices: 35.9 us -> none  [local(): lax.all_gather(scaled, 'cols', axis=0, tiled=True)]
    ppermute x2 -> x0, starting transfers between devices: 25.1 us -> none  [shifted(): return lax.ppermute(value, axis, pairs)]
    dot_general x9 -> x0, matrix products: 12.9 us -> none  [the longest x1 3.2 us: local(): jnp.dot(columns.T, agg_grad, precision=high)]
  transfers between devices with their start and end apart: 5 -> 0, of which waited for: 4 -> 0; matrix products, arithmetic and copies ran while one was open for 1% -> 0% of each run, Pallas kernels for 0% -> 0%
where the time goes in v1:
time: 79.7 us; the launch traced here: 79.5 us
  Pallas kernels  73.4 us (92%)
  local copies, waits for them, and re-layouts  4.8 us (6%)
  between operations  1.29 us (2%)
    pallas_call x1, Pallas kernels, local(): pl.pallas_call(kernel, out_shape=(jax.ShapeDtypeStruct((T, F), f32), jax....  73.4 us
    unnamed x3, local copies, waits for them, and re-layouts  4.8 us

profile of v1, /device:TPU:1, one launch (start us, length us, event | category | flops | bytes accessed | tf_op | source)
XLA Modules:
  0.0 79.5 jit_solution(4213444385525876407)
XLA Ops:
  1.3 73.4 %layer.1 = (f32[128,256]{1,0:T(8,128)}, f32[128,256]{1,0:T(8,128)}, f32[32,8,256]{2,1,0:T(8,128)}) custom-call(s32[1,128]{1,0:T(1,128)} %bitcast.5, s32[1,24]{1,0:T(1,128)} %coords.1, s32[1]{0:T(128)S(6)} %copy.13.counts, f32[128,256]{1,0:T(8,128)} %feat.1, f32[24,128,128]{2,1,0:T(8,128)} %bitcast.3, f32[256,256]{1,0:T(8,128)} %weight.1, f32[128,256]{1,0:T(8,128)} %cot.1), custom_call_target="tpu_custom_call" | custom-call | flops 400000000 | bytes 3000000 | tf_op jit(solution)/shard_map/layer/pallas_call | solution.py:281
  74.7 1.6 %copy.14 = f32[128,256]{1,0:T(8,128)} copy(f32[128,256]{1,0:T(8,128)} %get-tuple-element.12) | data formatting | bytes 262144
  76.2 1.6 %copy.15 = f32[128,256]{1,0:T(8,128)} copy(f32[128,256]{1,0:T(8,128)} %get-tuple-element.13) | data formatting | bytes 262144
  77.8 1.7 %copy.16 = f32[256,256]{1,0:T(8,128)} copy(f32[256,256]{1,0:T(8,128)} %bitcast.4) | data formatting | bytes 524288

commit v2 on v1

--- a/solution.py
+++ b/solution.py
@@ -15,6 +15,8 @@
 f32 = jnp.float32
 
 PLANE = [(h, x, y) for h in range(2) for x in range(4) for y in range(2) if (h, x, y) != (0, 0, 0)]
+PLANE.sort(key=lambda p: -(2 * p[0] + min(p[1], 4 - p[1]) + (p[2] if not p[0] else 0)))
+FAR = [4, 3, 5, 2, 6, 1, 7]
 CHIPS = [(x, y) for x in range(4) for y in range(2) if (x, y) != (0, 0)]
 
 
@@ -23,13 +25,13 @@
 
 
 def kernel(
-    deg, coords, counts, feat, tiles, weight, cot,
+    deg_i, coords_i, counts_i, feat, tiles, weight, cot,
     hid_o, fg_o, wg_o,
-    X, XN, TV, A, FV, WV, CV, NB, AGG, PG, G, HID,
+    deg, coords, counts, X, XN, TV, A, FV, WV, CV, NB, AGG, PG, G, HID,
     WP, WR, WS, R1, ZA, ZB, FW,
     TS, TO, RB, RC, TN, RN, FGV,
     lsem, xsend, xrecv, nsend, nrecv, wsend, wrecv, psend, precv,
-    zasend, zarecv, zbsend, zbrecv, fsend, frecv, tsend, trecv, csend, crecv, osem, chain,
+    zasend, zarecv, zbsend, zbrecv, fsend, frecv, tsend, trecv, csend, crecv, osem, chain, pchain,
 ):
     r = lax.axis_index("rows")
     c = lax.axis_index("cols")
@@ -65,16 +67,22 @@
         pltpu.make_async_copy(tiles, TV, lsem.at[1]),
         pltpu.make_async_copy(weight, WV, lsem.at[2]),
         pltpu.make_async_copy(cot, CV, lsem.at[3]),
+        pltpu.make_async_copy(deg_i, deg, lsem.at[4]),
+        pltpu.make_async_copy(coords_i, coords, lsem.at[5]),
+        pltpu.make_async_copy(counts_i, counts, lsem.at[6]),
     ]
-    for cp in loads:
-        cp.start()
+    for i in (4, 0):
+        loads[i].start()
 
     barrier = pltpu.get_barrier_semaphore()
-    greet = [dev(dh=a, dx=b, dy=d) for a, b, d in PLANE]
-    greet += [SIB, nxt, prv, dev(dz=1), dev(dz=31)]
+    R, L, Y, H = dev(dx=1), dev(dx=3), dev(dy=1), dev(dh=1)
+    greet = [H, R, L, Y, nxt, prv, dev(dz=1), dev(dz=31), SIB]
     for to in greet:
         pl.semaphore_signal(barrier, inc=1, device_id=to, device_id_type=MESH)
 
+    for i in (1, 5, 6, 2, 3):
+        loads[i].start()
+    loads[4].wait()
     nrow = 1.0 / jnp.sqrt(deg[...].astype(f32))
     eye = lax.broadcasted_iota(jnp.int32, (T, T), 0) == lax.broadcasted_iota(jnp.int32, (T, T), 1)
     norm = jnp.sum(jnp.where(eye, jnp.broadcast_to(nrow, (T, T)), 0.0), axis=1, keepdims=True)
@@ -103,22 +111,35 @@
             for dz in (d, 32 - d):
                 pl.semaphore_signal(chain.at[level], inc=1, device_id=dev(dz=dz), device_id_type=MESH)
 
+    def plane_step(level):
+        if level > 0:
+            pl.semaphore_wait(pchain.at[level - 1], (4, 2)[level - 1])
+        if level < 2:
+            for to in ((R, L, Y, H), (dev(dh=1, dy=1), dev(dx=2)))[level]:
+                pl.semaphore_signal(pchain.at[level], inc=1, device_id=to, device_id_type=MESH)
+
+    def send_all(sl, to):
+        start(X.at[sl], X.at[sl], xsend.at[len(pending)], xrecv.at[sl, 0], to)
+
+    def recv_all(sl):
+        remote(X.at[sl], X.at[sl], xsend.at[0], xrecv.at[sl, 0], SIB).wait_recv()
+
     def use(sl):
         AGG[...] += dot(A[sl], X[sl])
 
-    R, L, Y = dev(dx=1), dev(dx=3), dev(dy=1)
     send(me, 0, Y)
     send(me, 1, Y)
     send(me, 0, R)
     send(me, 1, L)
     send(me, 1, R)
     send(me, 0, L)
-    for hf in (0, 1):
-        send(me, hf, SIB)
+    send_all(me, SIB)
     start(X.at[me], XN, nsend.at[0], nrecv.at[0], prv)
     step(0)
-
-    loads[1].wait()
+    plane_step(0)
+
+    for i in (1, 5, 6):
+        loads[i].wait()
     live = counts[0]
 
     def build(j, carry):
@@ -139,9 +160,7 @@
     send(ys, 1, L)
     send(ys, 1, R)
     send(ys, 0, L)
-    for hf in (0, 1):
-        send(ys, hf, SIB)
-    step(1)
+    send_all(ys, SIB)
     done = [ys]
     for dy in (0, 1):
         a, b = slot(dx=3, dy=dy), slot(dx=1, dy=dy)
@@ -149,13 +168,13 @@
         send(a, 0, R)
         recv(b, 1)
         send(b, 1, L)
-        send(a, 0, SIB)
-        send(b, 1, SIB)
         recv(a, 1)
-        send(a, 1, SIB)
+        send_all(a, SIB)
         recv(b, 0)
-        send(b, 0, SIB)
-        step(2 + dy)
+        send_all(b, SIB)
+        step(1 + dy)
+        if dy == 0:
+            plane_step(1)
         for sl in done:
             use(sl)
         done = [a, b]
@@ -165,14 +184,18 @@
             recv(sl, hf)
             send(sl, hf, SIB)
         done.append(sl)
+    step(3)
     for sl in done:
         use(sl)
     remote(X.at[me], XN, nsend.at[0], nrecv.at[0], prv).wait_recv()
     AGG[...] += dot(A[NCOLS], XN[...])
     for dx, dy in [(0, 0), (0, 1), (3, 0), (1, 0), (3, 1), (1, 1), (2, 0), (2, 1)]:
         sl = slot(dx=dx, dy=dy, dc=1)
-        for hf in (0, 1):
-            recv(sl, hf)
+        if dx == 2:
+            for hf in (0, 1):
+                recv(sl, hf)
+        else:
+            recv_all(sl)
         use(sl)
 
     loads[2].wait()
@@ -198,6 +221,7 @@
     def plane_id(dh=0, dx=0, dy=0):
         return ((x + dx) % 4) * 4 + ((h + dh) % 2) * 2 + (y + dy) % 2
 
+    plane_step(2)
     q = plane_id()
     for i, (a, b, d) in enumerate(PLANE):
         start(WS.at[plane_id(a, b, d)], R1.at[i], psend.at[i], precv.at[i], dev(dh=a, dx=b, dy=d))
@@ -215,7 +239,7 @@
         total = total + R1[i]
     z4, zs = z % 4, z // 4
     ZA[z4] = total
-    for i in range(1, 4):
+    for i in (2, 3, 1):
         m = (z4 + i) % 4
         start(ZA.at[z4], ZA.at[z4], zasend.at[i - 1], zarecv.at[z4], (h * 32 + zs * 4 + m, c))
     step(4)
@@ -226,7 +250,7 @@
         m = (z4 + i) % 4
         remote(ZA.at[m], ZA.at[m], zasend.at[0], zarecv.at[m], SIB).wait_recv()
     ZB[zs] = ((ZA[0] + ZA[1]) + (ZA[2] + ZA[3]))
-    for i in range(1, 8):
+    for i in FAR:
         start(ZB.at[zs], ZB.at[zs], zbsend.at[i - 1], zbrecv.at[zs], dev(dz=4 * i))
 
     cp_id = x * 2 + y
@@ -240,10 +264,12 @@
     total = ZB[0]
     for i in range(1, 8):
         total = total + ZB[i]
-    FW[k * 16 + q] = total
-    mine = FW.at[k * 16 + q]
+    FW[...] = total
+    own = pltpu.make_async_copy(FW, wg_o.at[k * 16 + q], osem.at[2])
+    own.start()
+    mine = wg_o.at[k * 16 + q]
     for i, (a, b, d) in enumerate(PLANE):
-        start(mine, mine, fsend.at[i], frecv.at[q], dev(dh=a, dx=b, dy=d))
+        start(FW, mine, fsend.at[i], frecv.at[q], dev(dh=a, dx=b, dy=d))
 
     remote(TN, RN, nsend.at[1], nrecv.at[1], nxt).wait_recv()
     for i in range(7):
@@ -257,44 +283,37 @@
 
     for a, b, d in PLANE:
         o = plane_id(a, b, d)
-        part = FW.at[k * 16 + o]
+        part = wg_o.at[k * 16 + o]
         remote(part, part, fsend.at[0], frecv.at[o], SIB).wait_recv()
-    block = FW.at[pl.ds(k * 16, 16)]
+    own.wait()
+    block = wg_o.at[pl.ds(k * 16, 16)]
     start(block, block, wsend.at[1], wrecv.at[1], SIB)
-    other = FW.at[pl.ds((1 - k) * 16, 16)]
+    other = wg_o.at[pl.ds((1 - k) * 16, 16)]
     remote(other, other, wsend.at[1], wrecv.at[1], SIB).wait_recv()
-    wg_copy = pltpu.make_async_copy(FW, wg_o, osem.at[2])
-    wg_copy.start()
     hid_copy.wait()
     fg_copy.wait()
     for cp in pending:
         cp.wait_send()
-    wg_copy.wait()
 
 
 def local(features, degrees, tiles, coords, counts, weight, cotangent):
     anyspace = pl.BlockSpec(memory_space=pl.ANY)
-    smem = pl.BlockSpec(memory_space=pltpu.SMEM)
-    vmem = pl.BlockSpec(memory_space=pltpu.VMEM)
     D = pltpu.SemaphoreType.DMA
     V = lambda *s: pltpu.VMEM(s, f32)
     hidden, feature_grad, weight_grad = pl.pallas_call(
         kernel,
-        out_shape=(
-            jax.ShapeDtypeStruct((T, F), f32),
-            jax.ShapeDtypeStruct((T, F), f32),
-            jax.ShapeDtypeStruct((32, 8, F), f32),
-        ),
-        in_specs=[vmem, smem, smem, anyspace, anyspace, anyspace, anyspace],
+        out_shape=(pltpu.VMEM((T, F), f32), pltpu.VMEM((T, F), f32), pltpu.VMEM((32, 8, F), f32)),
+        in_specs=[pl.BlockSpec(memory_space=pltpu.HBM)] * 7,
         out_specs=(anyspace, anyspace, anyspace),
         scratch_shapes=[
+            pltpu.VMEM((1, T), jnp.int32), pltpu.SMEM((1, SLOTS), jnp.int32), pltpu.SMEM((1,), jnp.int32),
             V(NCOLS, T, F), V(T, F), V(SLOTS, T, T), V(NCOLS + 1, T, T), V(T, F), V(F, F), V(T, F),
             V(T, F), V(T, F), V(T, F), V(T, F), V(T, F),
-            V(2, T, F), V(T, F), V(16, 8, F), V(15, 8, F), V(4, 8, F), V(8, 8, F), V(32, 8, F),
+            V(2, T, F), V(T, F), V(16, 8, F), V(15, 8, F), V(4, 8, F), V(8, 8, F), V(8, F),
             V(8, T, F), V(8, T, F), V(8, T, F), V(7, T, F), V(T, F), V(T, F), V(T, F),
-            D((4,)), D((48,)), D((NCOLS, 2)), D((2,)), D((2,)), D((2,)), D((2,)), D((15,)), D((15,)),
+            D((7,)), D((48,)), D((NCOLS, 2)), D((2,)), D((2,)), D((2,)), D((2,)), D((15,)), D((15,)),
             D((3,)), D((4,)), D((7,)), D((8,)), D((15,)), D((16,)), D((8,)), D((8,)), D((7,)), D((7,)),
-            D((3,)), pltpu.SemaphoreType.REGULAR((4,)),
+            D((3,)), pltpu.SemaphoreType.REGULAR((4,)), pltpu.SemaphoreType.REGULAR((2,)),
         ],
         compiler_params=pltpu.CompilerParams(
             collective_id=1, has_side_effects=True, vmem_limit_bytes=60 << 20

time: 79.7 us -> 75.3 us (0.945)
  local copies, waits for them, and re-layouts: 4.8 us -> 2.01 us
  Pallas kernels: 73.4 us -> 71.8 us
    unnamed x3, local copies, waits for them, and re-layouts: 4.8 us -> 2.01 us
    pallas_call x1, Pallas kernels: 73.4 us -> 71.8 us  [local(): pl.pallas_call(kernel, out_shape=(pltpu.VMEM((T, F), f32), pltpu.VMEM((T,...]
where the time goes in v2:
time: 75.3 us; the launch traced here: 75.1 us
  Pallas kernels  71.8 us (95%)
  local copies, waits for them, and re-layouts  2.01 us (3%)
  between operations  1.29 us (2%)
    pallas_call x1, Pallas kernels, local(): pl.pallas_call(kernel, out_shape=(pltpu.VMEM((T, F), f32), pltpu.VMEM((T,...  71.8 us
    unnamed x3, local copies, waits for them, and re-layouts  2.01 us

profile of v2, /device:TPU:1, one launch (start us, length us, event | category | flops | bytes accessed | tf_op | source)
XLA Modules:
  0.0 75.1 jit_solution(4446211761424140781)
XLA Ops:
  1.3 71.8 %layer.1 = (f32[128,256]{1,0:T(8,128)S(1)}, f32[128,256]{1,0:T(8,128)S(1)}, f32[32,8,256]{2,1,0:T(8,128)S(1)}) custom-call(s32[1,128]{1,0:T(1,128)} %bitcast.5, s32[1,24]{1,0:T(1,128)} %coords_i.1, s32[1]{0:T(128)S(6)} %copy.16.counts_i, f32[128,256]{1,0:T(8,128)} %feat.1, f32[24,128,128]{2,1,0:T(8,128)} %bitcast.4, f32[256,256]{1,0:T(8,128)} %weight.1, ...), custom_call_target="tpu_custom_call" | custom-call | flops 400000000 | bytes 3000000 | tf_op jit(solution)/shard_map/layer/pallas_call | solution.py:303
  73.1 0.7 copy.13
  73.8 0.7 copy.14
  74.4 0.7 copy.15

commit v3 on v2

--- a/solution.py
+++ b/solution.py
@@ -10,7 +10,6 @@
 SLOTS = 24
 ROWS = 64
 NCOLS = 16
-HIGH = lax.Precision.HIGHEST
 MESH = pl.DeviceIdType.MESH
 f32 = jnp.float32
 
@@ -20,14 +19,22 @@
 CHIPS = [(x, y) for x in range(4) for y in range(2) if (x, y) != (0, 0)]
 
 
+def split(v):
+    top = v.astype(jnp.bfloat16)
+    return top, (v - top.astype(f32)).astype(jnp.bfloat16)
+
+
 def dot(a, b, ca=1, cb=0):
-    return lax.dot_general(a, b, (((ca,), (cb,)), ((), ())), precision=HIGH, preferred_element_type=f32)
+    def one(u, v):
+        return lax.dot_general(u, v, (((ca,), (cb,)), ((), ())), preferred_element_type=f32)
+
+    return one(a[0], b[0]) + (one(a[0], b[1]) + one(a[1], b[0]))
 
 
 def kernel(
     deg_i, coords_i, counts_i, feat, tiles, weight, cot,
     hid_o, fg_o, wg_o,
-    deg, coords, counts, X, XN, TV, A, FV, WV, CV, NB, AGG, PG, G, HID,
+    deg, coords, counts, X, XN, TV, A1, A2, FV, WV, CV, NB, AGG, W1, W2, G1, G2, HID,
     WP, WR, WS, R1, ZA, ZB, FW,
     TS, TO, RB, RC, TN, RN, FGV,
     lsem, xsend, xrecv, nsend, nrecv, wsend, wrecv, psend, precv,
@@ -57,6 +64,11 @@
         cp = remote(src, dst, ss, rs, to)
         cp.start()
         pending.append(cp)
+
+    def settle(count):
+        for cp in pending[-count:]:
+            cp.wait_send()
+        del pending[-count:]
 
     SIB = dev(dc=1)
     nxt = ((r + 1) % ROWS, c)
@@ -124,8 +136,11 @@
     def recv_all(sl):
         remote(X.at[sl], X.at[sl], xsend.at[0], xrecv.at[sl, 0], SIB).wait_recv()
 
+    def block(j):
+        return A1[j], A2[j]
+
     def use(sl):
-        AGG[...] += dot(A[sl], X[sl])
+        AGG[...] += dot(block(sl), split(X[sl]))
 
     send(me, 0, Y)
     send(me, 1, Y)
@@ -147,11 +162,14 @@
         for t in range(SLOTS):
             on = jnp.logical_and(coords[0, t] == j, t < live)
             acc = acc + jnp.where(on, 1.0, 0.0) * TV[t]
-        A[j] = acc
+        A1[j], A2[j] = split(acc)
         return carry
 
     lax.fori_loop(0, NCOLS + 1, build, 0)
-    AGG[...] = dot(A[me], X[me])
+    AGG[...] = dot(block(me), split(X[me]))
+    loads[2].wait()
+    W1[...], W2[...] = split(WV[...])
+    loads[3].wait()
 
     ys = slot(dy=1)
     recv(ys, 0)
@@ -188,7 +206,7 @@
     for sl in done:
         use(sl)
     remote(X.at[me], XN, nsend.at[0], nrecv.at[0], prv).wait_recv()
-    AGG[...] += dot(A[NCOLS], XN[...])
+    AGG[...] += dot(block(NCOLS), split(XN[...]))
     for dx, dy in [(0, 0), (0, 1), (3, 0), (1, 0), (3, 1), (1, 1), (2, 0), (2, 1)]:
         sl = slot(dx=dx, dy=dy, dc=1)
         if dx == 2:
@@ -198,25 +216,24 @@
             recv_all(sl)
         use(sl)
 
-    loads[2].wait()
-    loads[3].wait()
     agg = AGG[...] * NB[...]
-    pre = dot(agg, WV[...])
+    wparts = W1[...], W2[...]
+    pre = dot(split(agg), wparts)
     gate = jax.nn.sigmoid(pre)
+    pg = split(CV[...] * gate * (1.0 + pre * (1.0 - gate)))
+    first, second = split(agg[:, :T]), split(agg[:, T:])
+    theirs = [jnp.where(k == 0, u, v) for u, v in zip(second, first)]
+    own = [jnp.where(k == 0, u, v) for u, v in zip(first, second)]
+    WP[...] = dot(theirs, pg, 0, 0)
+    start(WP, WR, wsend.at[0], wrecv.at[0], SIB)
+    mine = dot(own, pg, 0, 0)
     HID[...] = pre * gate
     hid_copy = pltpu.make_async_copy(HID, hid_o, osem.at[0])
     hid_copy.start()
-    pg = CV[...] * gate * (1.0 + pre * (1.0 - gate))
-    PG[...] = pg
-    wg = dot(agg, pg, 0, 0)
-    WP[0] = wg[:T]
-    WP[1] = wg[T:]
-    start(WP.at[1 - k], WR, wsend.at[0], wrecv.at[0], SIB)
-    G[...] = dot(PG[...], WV[...], 1, 1) * NB[...]
-    TN[...] = dot(A[NCOLS], G[...], 0, 0)
-    start(TN, RN, nsend.at[1], nrecv.at[1], nxt)
-    remote(WP.at[0], WR, wsend.at[0], wrecv.at[0], SIB).wait_recv()
-    WS[...] = (WP[k] + WR[...]).reshape(16, 8, F)
+    g = split(dot(pg, wparts, 1, 1) * NB[...])
+    G1[...], G2[...] = g
+    remote(WP, WR, wsend.at[0], wrecv.at[0], SIB).wait_recv()
+    WS[...] = (mine + WR[...]).reshape(16, 8, F)
 
     def plane_id(dh=0, dx=0, dy=0):
         return ((x + dx) % 4) * 4 + ((h + dh) % 2) * 2 + (y + dy) % 2
@@ -226,11 +243,17 @@
     for i, (a, b, d) in enumerate(PLANE):
         start(WS.at[plane_id(a, b, d)], R1.at[i], psend.at[i], precv.at[i], dev(dh=a, dx=b, dy=d))
 
+    def term(j):
+        return dot(block(j), (G1[...], G2[...]), 0, 0)
+
+    TN[...] = term(NCOLS)
     for p in range(8):
-        TS[p] = dot(A[p * 2 + 1 - k], G[...], 0, 0)
+        TS[p] = term(p * 2 + 1 - k)
+    for p in range(8):
+        TO[p] = term(p * 2 + k)
+    start(TN, RN, nsend.at[1], nrecv.at[1], nxt)
+    for p in range(8):
         start(TS.at[p], RB.at[p], tsend.at[p], trecv.at[p], SIB)
-    for p in range(8):
-        TO[p] = dot(A[p * 2 + k], G[...], 0, 0)
 
     for i in range(15):
         remote(WS.at[0], R1.at[i], psend.at[i], precv.at[i], SIB).wait_recv()
@@ -243,16 +266,18 @@
         m = (z4 + i) % 4
         start(ZA.at[z4], ZA.at[z4], zasend.at[i - 1], zarecv.at[z4], (h * 32 + zs * 4 + m, c))
     step(4)
-    for p in range(8):
-        remote(TS.at[p], RB.at[p], tsend.at[p], trecv.at[p], SIB).wait_recv()
-        TO[p] = TO[p] + RB[p]
     for i in range(1, 4):
         m = (z4 + i) % 4
         remote(ZA.at[m], ZA.at[m], zasend.at[0], zarecv.at[m], SIB).wait_recv()
     ZB[zs] = ((ZA[0] + ZA[1]) + (ZA[2] + ZA[3]))
     for i in FAR:
-        start(ZB.at[zs], ZB.at[zs], zbsend.at[i - 1], zbrecv.at[zs], dev(dz=4 * i))
-
+        m = 3 - z4 if i == 4 else z4
+        to = (h * 32 + ((zs + i) % 8) * 4 + m, c)
+        start(ZB.at[zs], ZB.at[zs], zbsend.at[i - 1], zbrecv.at[zs], to)
+
+    for p in range(8):
+        remote(TS.at[p], RB.at[p], tsend.at[p], trecv.at[p], SIB).wait_recv()
+        TO[p] = TO[p] + RB[p]
     cp_id = x * 2 + y
     for i, (dx, dy) in enumerate(CHIPS):
         to = ((x + dx) % 4) * 2 + (y + dy) % 2
@@ -265,8 +290,8 @@
     for i in range(1, 8):
         total = total + ZB[i]
     FW[...] = total
-    own = pltpu.make_async_copy(FW, wg_o.at[k * 16 + q], osem.at[2])
-    own.start()
+    own_copy = pltpu.make_async_copy(FW, wg_o.at[k * 16 + q], osem.at[2])
+    own_copy.start()
     mine = wg_o.at[k * 16 + q]
     for i, (a, b, d) in enumerate(PLANE):
         start(FW, mine, fsend.at[i], frecv.at[q], dev(dh=a, dx=b, dy=d))
@@ -285,9 +310,9 @@
         o = plane_id(a, b, d)
         part = wg_o.at[k * 16 + o]
         remote(part, part, fsend.at[0], frecv.at[o], SIB).wait_recv()
-    own.wait()
-    block = wg_o.at[pl.ds(k * 16, 16)]
-    start(block, block, wsend.at[1], wrecv.at[1], SIB)
+    own_copy.wait()
+    part = wg_o.at[pl.ds(k * 16, 16)]
+    start(part, part, wsend.at[1], wrecv.at[1], SIB)
     other = wg_o.at[pl.ds((1 - k) * 16, 16)]
     remote(other, other, wsend.at[1], wrecv.at[1], SIB).wait_recv()
     hid_copy.wait()
@@ -296,10 +321,19 @@
         cp.wait_send()
 
 
+def deliver(a, b, c, ao, bo, co, sem):
+    copies = [pltpu.make_async_copy(i, o, sem.at[n]) for n, (i, o) in enumerate(((a, ao), (b, bo), (c, co)))]
+    for cp in copies:
+        cp.start()
+    for cp in copies:
+        cp.wait()
+
+
 def local(features, degrees, tiles, coords, counts, weight, cotangent):
     anyspace = pl.BlockSpec(memory_space=pl.ANY)
     D = pltpu.SemaphoreType.DMA
     V = lambda *s: pltpu.VMEM(s, f32)
+    B = lambda *s: pltpu.VMEM(s, jnp.bfloat16)
     hidden, feature_grad, weight_grad = pl.pallas_call(
         kernel,
         out_shape=(pltpu.VMEM((T, F), f32), pltpu.VMEM((T, F), f32), pltpu.VMEM((32, 8, F), f32)),
@@ -307,9 +341,9 @@
         out_specs=(anyspace, anyspace, anyspace),
         scratch_shapes=[
             pltpu.VMEM((1, T), jnp.int32), pltpu.SMEM((1, SLOTS), jnp.int32), pltpu.SMEM((1,), jnp.int32),
-            V(NCOLS, T, F), V(T, F), V(SLOTS, T, T), V(NCOLS + 1, T, T), V(T, F), V(F, F), V(T, F),
-            V(T, F), V(T, F), V(T, F), V(T, F), V(T, F),
-            V(2, T, F), V(T, F), V(16, 8, F), V(15, 8, F), V(4, 8, F), V(8, 8, F), V(8, F),
+            V(NCOLS, T, F), V(T, F), V(SLOTS, T, T), B(NCOLS + 1, T, T), B(NCOLS + 1, T, T), V(T, F), V(F, F), V(T, F),
+            V(T, F), V(T, F), B(F, F), B(F, F), B(T, F), B(T, F), V(T, F),
+            V(T, F), V(T, F), V(16, 8, F), V(15, 8, F), V(4, 8, F), V(8, 8, F), V(8, F),
             V(8, T, F), V(8, T, F), V(8, T, F), V(7, T, F), V(T, F), V(T, F), V(T, F),
             D((7,)), D((48,)), D((NCOLS, 2)), D((2,)), D((2,)), D((2,)), D((2,)), D((15,)), D((15,)),
             D((3,)), D((4,)), D((7,)), D((8,)), D((15,)), D((16,)), D((8,)), D((8,)), D((7,)), D((7,)),
@@ -321,6 +355,16 @@
         cost_estimate=pl.CostEstimate(flops=400_000_000, bytes_accessed=3_000_000, transcendentals=32768),
         name="layer",
     )(degrees.reshape(1, T), coords, counts, features, tiles.reshape(SLOTS, T, T), weight, cotangent)
+    shapes = [(T, F), (T, F), (32, 8, F)]
+    outs = [pltpu.with_memory_space_constraint(v, pltpu.VMEM) for v in (hidden, feature_grad, weight_grad)]
+    hidden, feature_grad, weight_grad = pl.pallas_call(
+        deliver,
+        out_shape=tuple(jax.ShapeDtypeStruct(s, f32) for s in shapes),
+        in_specs=[anyspace] * 3,
+        out_specs=(anyspace,) * 3,
+        scratch_shapes=[D((3,))],
+        name="deliver",
+    )(*outs)
     return hidden, feature_grad, weight_grad.reshape(F, F)
 
 

time: 75.3 us -> 70.5 us (0.936)
  Pallas kernels: 71.8 us -> 69.1 us
  local copies, waits for them, and re-layouts: 2.01 us -> 0 us
    pallas_call x1, Pallas kernels: 71.8 us -> 68.2 us  [local(): pl.pallas_call(kernel, out_shape=(pltpu.VMEM((T, F), f32), pltpu.VMEM((T,...]
    unnamed x3 -> x0, local copies, waits for them, and re-layouts: 2.01 us -> none
    pallas_call x0 -> x1, Pallas kernels: none -> 0.82 us  [local(): pl.pallas_call(deliver, out_shape=tuple((jax.ShapeDtypeStruct(s, f32) for...]
where the time goes in v3:
time: 70.5 us; the launch traced here: 70.4 us
  Pallas kernels  69.1 us (98%)
  between operations  1.29 us (2%)
    pallas_call x1, Pallas kernels, local(): pl.pallas_call(kernel, out_shape=(pltpu.VMEM((T, F), f32), pltpu.VMEM((T,...  68.2 us

profile of v3, /device:TPU:1, one launch (start us, length us, event | category | flops | bytes accessed | tf_op | source)
XLA Modules:
  0.0 70.4 jit_solution(6931519402664559124)
XLA Ops:
  1.3 68.2 %layer.1 = (f32[128,256]{1,0:T(8,128)S(1)}, f32[128,256]{1,0:T(8,128)S(1)}, f32[32,8,256]{2,1,0:T(8,128)S(1)}) custom-call(s32[1,128]{1,0:T(1,128)} %bitcast.4, s32[1,24]{1,0:T(1,128)} %coords_i.1, s32[1]{0:T(128)S(6)} %copy.10.counts_i, f32[128,256]{1,0:T(8,128)} %feat.1, f32[24,128,128]{2,1,0:T(8,128)} %bitcast.3, f32[256,256]{1,0:T(8,128)} %weight.1, ...), custom_call_target="tpu_custom_call" | custom-call | flops 400000000 | bytes 3000000 | tf_op jit(solution)/shard_map/layer/pallas_call | solution.py:337
  69.5 0.8 %deliver.1 = (f32[128,256]{1,0:T(8,128)}, f32[128,256]{1,0:T(8,128)}, f32[32,8,256]{2,1,0:T(8,128)}) custom-call(f32[128,256]{1,0:T(8,128)S(1)} %get-tuple-element.9.a, f32[128,256]{1,0:T(8,128)S(1)} %get-tuple-element.10.b, f32[32,8,256]{2,1,0:T(8,128)S(1)} %get-tuple-element.11.c), custom_call_target="tpu_custom_call" | custom-call | tf_op jit(solution)/shard_map/deliver/pallas_call | solution.py:360
